TPU v7x, 256 devices: a whole 4x4x8 slice. The times are simulated.
256 devices in a mesh: keys: 64 (over y, z, core), seq: 4 (over x).
Axes of the slice: x: 4, y: 4, z: 8, core: 2. Of those that a mesh axis runs over, the one named last changes fastest.
Arguments:
- span_queries: bfloat16 [1536, 768], P(('keys', 'seq')), may hold values from -6 to 6
- key_slab: bfloat16 [4096, 768], P('keys'), may hold values from -0.21875 to 0.21875
- neighbour_store: bfloat16 [4096, 64, 896], P('keys'), may hold values from -6 to 6
- neighbour_ids: int32 [1536, 2], P(('keys', 'seq')), may hold values from 0 to 4094, as said below
- attn_queries: bfloat16 [98304, 2048], P(('keys', 'seq')), may hold values from -200 to 200
- kv_weight: bfloat16 [2, 2048, 896], P(None, 'keys'), may hold values from -0.1875 to 0.1875
Outputs:
- best_scores: float32 [1536, 2], P(('keys', 'seq'))
- attended: bfloat16 [98304, 2048], P(('keys', 'seq'))
Inputs may be any that keep to these rules, and one draw needn't show every extreme that they name: `neighbour_ids`: each id c has c mod 64 at most 62, so c + 1 lies on the same shard c // 64. Among the 12 ids of one device's spans (aligned blocks of 6 rows), no shard holds more than 1, and some shard holds exactly 1.
All inputs are finite; a program needn't handle non-finite values.
Results may differ from a plain program's by a relative error of at most 0.012.
The roundings to bfloat16 on the way count: a program that leaves them out, or rounds other values in their place, can miss the bound.
Values may be sent and summed in bfloat16 or wider, within the bound.
A program may use at most 128 MiB of HBM per device.

v0:
```python
import jax
import jax.numpy as jnp
from jax import lax
from jax.sharding import PartitionSpec as P

HEADS = 16
HEAD_DIM = 128


def merged(part, axis, combine):
    gathered = jax.tree.map(lambda a: lax.all_gather(a, axis), part)

    def take(source):
        return jax.tree.map(lambda a: lax.dynamic_index_in_dim(a, source, 0, False), gathered)

    return lax.fori_loop(
        1, lax.axis_size(axis), lambda source, state: combine(state, take(source)), take(0)
    )


def keep_two(left, right):
    higher = jnp.maximum(left[0], right[0])
    runner = jnp.maximum(jnp.minimum(left[0], right[0]), jnp.maximum(left[1], right[1]))
    return (higher, runner)


def best_two(values):
    padding = jnp.full((values.shape[0], 2), -jnp.inf, values.dtype)
    return lax.top_k(jnp.concatenate([values, padding], axis=1), 2)[0]


def row_scores(left, right):
    return lax.dot_general(
        left, right, (((1,), (1,)), ((), ())), preferred_element_type=jnp.float32
    )


def body(span_queries, key_slab, neighbour_store, neighbour_ids, attn_queries, kv_weight):
    key_count = lax.axis_size("keys")
    position = lax.axis_index("keys")
    own_spans = neighbour_ids.shape[0]
    shard_spans = neighbour_store.shape[0]
    span_rows = neighbour_store.shape[1]
    enc_width = neighbour_store.shape[2]
    candidates = best_two(
        row_scores(lax.all_gather(span_queries, "keys", axis=0, tiled=True), key_slab)
    )
    higher_all, runner_all = merged((candidates[:, 0], candidates[:, 1]), "keys", keep_two)
    higher = lax.dynamic_slice_in_dim(higher_all, position * own_spans, own_spans)
    runner = lax.dynamic_slice_in_dim(runner_all, position * own_spans, own_spans)
    best_scores = jnp.stack([higher, runner], axis=1)
    flat_ids = neighbour_ids.reshape(-1)
    need_count = flat_ids.shape[0]
    per_shard = (need_count + key_count - 1) // key_count
    capacity = 2 * per_shard
    target = flat_ids // shard_spans
    offset = flat_ids % shard_spans
    order_index = jnp.arange(need_count, dtype=jnp.int32)
    same_shard = (target[:, None] == target[None, :]) & (
        order_index[:, None] < order_index[None, :]
    )
    slot_base = 2 * jnp.sum(same_shard.astype(jnp.int32), axis=0)
    slot_index = jnp.arange(capacity, dtype=jnp.int32)
    shard_onehot = (target[:, None] == jnp.arange(key_count, dtype=jnp.int32)[None, :]).astype(
        jnp.int32
    )
    first_slot = (slot_index == slot_base[..., None]).astype(jnp.int32) * offset[..., None]
    next_slot = (slot_index == slot_base[..., None] + 1).astype(jnp.int32) * (offset[..., None] + 1)
    table = jnp.einsum("nj,ns->js", shard_onehot, first_slot + next_slot)
    incoming = lax.all_to_all(table, "keys", split_axis=0, concat_axis=0, tiled=True)
    outgoing = neighbour_store[incoming]
    arrived = lax.all_to_all(outgoing, "keys", split_axis=0, concat_axis=0, tiled=True)
    arrived = arrived.reshape(key_count * capacity, span_rows, enc_width)
    first_row = target * capacity + slot_base
    picked = arrived[jnp.stack([first_row, first_row + 1], axis=1)]
    neighbours = picked.reshape(own_spans * 4 * span_rows, enc_width)
    keys_values = jnp.einsum(
        "re,tce->rtc",
        neighbours,
        lax.all_gather(kv_weight, "keys", axis=1, tiled=True),
        preferred_element_type=jnp.float32,
    ).astype(jnp.bfloat16)
    key_rows = keys_values[:, 0].reshape(own_spans, 4 * span_rows, HEADS, HEAD_DIM)
    value_rows = keys_values[:, 1].reshape(own_spans, 4 * span_rows, HEADS, HEAD_DIM)
    queries = attn_queries.reshape(own_spans, span_rows, HEADS, HEAD_DIM)
    logits = jnp.einsum(
        "cqhd,ckhd->chqk", queries, key_rows, preferred_element_type=jnp.float32
    ) * HEAD_DIM ** (-0.5)
    largest = jnp.max(logits, axis=-1, keepdims=True)
    expo_terms = jnp.exp(logits - largest)
    weights = (expo_terms / jnp.sum(expo_terms, axis=-1, keepdims=True)).astype(jnp.bfloat16)
    output = jnp.einsum("chqk,ckhd->cqhd", weights, value_rows, preferred_element_type=jnp.float32)
    attended = output.astype(jnp.bfloat16).reshape(own_spans * span_rows, HEADS * HEAD_DIM)
    return (best_scores, attended)


def solution(mesh):
    return jax.shard_map(
        body,
        mesh=mesh,
        in_specs=(
            P(("keys", "seq"), None),
            P("keys", None),
            P("keys", None, None),
            P(("keys", "seq"), None),
            P(("keys", "seq"), None),
            P(None, "keys", None),
        ),
        out_specs=(P(("keys", "seq"), None), P(("keys", "seq"), None)),
        check_vma=False,
    )
```

profile of v0, /device:TPU:1, one launch (start us, length us, event | category | flops | bytes accessed | tf_op | source)
XLA Modules:
  0.0 606.9 jit_solution(17030885371384447195)
XLA Ops:
  7.2 0.0 copy-start
  7.2 0.8 copy.33
  8.0 0.1 reshape.394
  8.1 0.1 convert_reduce_fusion
  8.2 0.3 fusion.23
  8.5 22.2 %all_to_all.17 = s32[64,1,2]{2,1,0:T(1,128)S(1)} all-to-all(s32[64,1,2]{2,1,0:T(1,128)S(1)} %bitcast.81), channel_id=1, replica_groups=mesh['keys'=64,'seq'=4] {'keys'}, dimensions={0} | all-to-all | bytes 1024 | tf_op jit(solution)/shard_map/all_to_all | solution.py:70
  30.7 0.1 copy.35
  30.8 0.1 copy.36
  30.9 0.1 reshape.402
  31.1 11.8 %gather_fusion = bf16[128,64,896]{2,1,0:T(8,128)(2,1)} fusion(bf16[64,64,896]{2,1,0:T(8,128)(2,1)} %param.10, s32[1024]{0:T(1024)S(1)} %pad_clamp_fusion.1), kind=kCustom, calls=%fused_computation | custom fusion | bytes 29360640 | tf_op jit(solution)/shard_map/gather | solution.py:71
  42.9 0.0 copy-start.3
  42.9 6.4 %all-to-all-start.1 = ((bf16[64,2,64,896]{3,2,1,0:T(8,128)(2,1)}), bf16[64,2,64,896]{3,2,1,0:T(8,128)(2,1)}, u32[]{:S(2)}, u32[]{:S(2)}) async-start(bf16[64,2,64,896]{3,2,1,0:T(8,128)(2,1)} %bitcast.73), calls=%async_computation.1 | async-start | bytes 29360128 | tf_op jit(solution)/shard_map/all_to_all | solution.py:72
  49.3 0.0 all-gather.5.cloned.1.call-start
  49.4 0.7 all-gather.5.cloned.1.call-update
  50.1 0.1 reshape.396
  50.2 0.1 copy.38
  50.3 0.1 reshape.410
  50.4 0.0 copy-done.3
  50.4 1.6 copy.44
  51.9 0.0 copy-done.4
  51.9 380.2 %all-gather.2 = bf16[64,6,768]{2,1,0:T(8,128)(2,1)S(1)} all-gather(bf16[1,6,768]{2,1,0:T(8,128)(2,1)S(1)} %bitcast.82), channel_id=1, replica_groups=mesh['keys'=64,'seq'=4] {'keys'}, dimensions={0}, use_global_device_ids=true | all-gather | bytes 599040 | tf_op jit(solution)/shard_map/all_gather | solution.py:46
  432.1 0.2 reshape.426
  432.3 0.0 copy-done
  432.3 0.3 fusion.43
  432.6 5.0 top_k.8
  437.7 48.6 %all-gather = f32[24576,1]{0,1:T(1,128)S(1)} all-gather(f32[384,1]{0,1:T(1,128)S(1)} %get-tuple-element.161), channel_id=2, replica_groups=mesh['keys'=64,'seq'=4] {'keys'}, dimensions={0}, use_global_device_ids=true | all-gather | bytes 99840 | tf_op jit(solution)/shard_map/all_gather | solution.py:11
  486.3 0.5 broadcast.499
  486.8 0.9 reduce.14
  487.7 44.4 %all-gather.1 = f32[24576,1]{0,1:T(1,128)S(1)} all-gather(f32[384,1]{0,1:T(1,128)S(1)} %get-tuple-element.160), channel_id=3, replica_groups=mesh['keys'=64,'seq'=4] {'keys'}, dimensions={0}, use_global_device_ids=true | all-gather | bytes 99840 | tf_op jit(solution)/shard_map/all_gather | solution.py:11
  532.2 0.9 reduce.15
  533.1 4.3 while.17
  537.4 0.1 dynamic-slice_bitcast_fusion
  537.5 0.6 pad_maximum_fusion
  538.1 0.0 all-to-all-done.1
  538.1 6.3 %gather_fusion.1 = bf16[24,64,896]{2,1,0:T(8,128)(2,1)S(1)} fusion(bf16[128,64,896]{2,1,0:T(8,128)(2,1)} %bitcast.6, s32[1024]{0:T(1024)S(1)} %pad_clamp_fusion), kind=kCustom, calls=%fused_computation.1 | custom fusion | bytes 5505120 | tf_op jit(solution)/shard_map/gather | solution.py:75
  544.4 0.0 all-gather.5.cloned.1.call-done
  544.4 18.7 %convolution_convert_fusion = bf16[1536,2,2048]{2,0,1:T(8,128)(2,1)} fusion(bf16[1536,896,1]{1,0,2:T(8,128)(2,1)S(1)} %bitcast.78, bf16[2,2048,896]{2,1,0:T(8,128)(2,1)} %all-gather.5.cloned.1.call-done), kind=kOutput, calls=%fused_computation.6 | convolution fusion | flops 11280580608 | bytes 22675456 | tf_op jit(solution)/shard_map/re,tce->rtc/dot_general | solution.py:77
  563.1 5.3 slice_bitcast_fusion.1
  568.4 2.3 copy.43
  570.8 3.7 fusion.5
  574.5 0.0 copy-start.2
  574.5 2.4 fusion.42
  576.9 5.0 copy.45
  581.9 0.0 copy-done.2
  581.9 15.5 %fusion.16 = bf16[6,64,16,128]{3,1,2,0:T(8,128)(2,1)S(1)} fusion(bf16[6,256,16,128]{3,2,1,0:T(8,128)(2,1)} %bitcast.75, f32[6,16,64]{2,1,0:T(8,128)S(1)} %fusion.42, f32[6,16,256,64]{2,3,1,0:T(8,128)} %copy-done.2), kind=kOutput, calls=%fused_computation.24 | convolution fusion | flops 411310336 | bytes 14180352 | tf_op jit(solution)/shard_map/chqk,ckhd->cqhd/dot_general | solution.py:92
  597.4 1.0 copy.42
  598.5 1.6 copy.58
  600.0 0.0 copy-done.1
  (142 shorter events, 2.7 us)
Async XLA Ops:
  7.2 425.1 %copy-start = (bf16[64,768]{1,0:T(8,128)(2,1)S(1)}, bf16[64,768]{1,0:T(8,128)(2,1)}, u32[]{:S(2)}) copy-start(bf16[64,768]{1,0:T(8,128)(2,1)} %param.9) | copy-start | bytes 294916
  42.9 7.4 %copy-start.3 = (bf16[384,2048]{1,0:T(8,128)(2,1)S(1)}, bf16[384,2048]{1,0:T(8,128)(2,1)}, u32[]{:S(2)}) copy-start(bf16[384,2048]{1,0:T(8,128)(2,1)} %param.12) | copy-start | bytes 4718596
  42.9 9.0 %copy-start.4 = (bf16[6,768]{1,0:T(8,128)(2,1)S(1)}, bf16[6,768]{1,0:T(8,128)(2,1)}, u32[]{:S(2)}) copy-start(bf16[6,768]{1,0:T(8,128)(2,1)} %param.8) | copy-start | bytes 27652
  42.9 495.2 %all-to-all-start.1 = ((bf16[64,2,64,896]{3,2,1,0:T(8,128)(2,1)}), bf16[64,2,64,896]{3,2,1,0:T(8,128)(2,1)}, u32[]{:S(2)}, u32[]{:S(2)}) async-start(bf16[64,2,64,896]{3,2,1,0:T(8,128)(2,1)} %bitcast.73), calls=%async_computation.1 | async-start | bytes 29360128 | tf_op jit(solution)/shard_map/all_to_all | solution.py:72
  49.3 495.1 %all-gather.5.cloned.1.call-start = ((), (), s32[]{:S(2)}) async-start(), calls=%async_computation.2 | async-start | bytes 7454720 | tf_op jit(solution)/shard_map/all_gather | solution.py:80
  574.5 7.4 %copy-start.2 = (f32[6,16,256,64]{2,3,1,0:T(8,128)}, f32[6,16,256,64]{2,3,1,0:T(8,128)S(1)}, u32[]{:S(2)}) copy-start(f32[6,16,256,64]{2,3,1,0:T(8,128)S(1)} %fusion.5) | copy-start | bytes 18874372
  581.9 18.1 %copy-start.1 = (bf16[64,768]{1,0:T(8,128)(2,1)S(1)}, bf16[64,768]{1,0:T(8,128)(2,1)}, u32[]{:S(2)}) copy-start(bf16[64,768]{1,0:T(8,128)(2,1)} %param.9) | copy-start | bytes 294916
Sparse Core Ops, SparseCore 0:
  53.0 126.6 all-gather.4
where the time goes:
time: 607 us
  blocking collectives  495 us (82%)
  local copies, waits for them, and re-layouts  38.9 us (6%)
  matrix products  38.6 us (6%)
  between operations  14.2 us (2%)
  other arithmetic  10.8 us (2%)
  starting transfers between devices  6.45 us (1%)
    all_gather x1, blocking collectives, body(): lax.all_gather(span_queries, 'keys', axis=0, tiled=True)  380 us
    all_gather x2, blocking collectives, merged(): gathered = jax.tree.map(lambda a: lax.all_gather(a, axis), part)  93 us
    all_to_all x1, blocking collectives, body(): lax.all_to_all(table, 'keys', split_axis=0, concat_axis=0, tiled=True)  22.2 us
    dot_general x1, matrix products, body(): jnp.einsum('re,tce->rtc', neighbours, lax.all_gather(kv_weight, 'keys', a...  18.7 us
    unnamed x17, local copies, waits for them, and re-layouts  16.8 us
    dot_general x1, matrix products, body(): jnp.einsum('chqk,ckhd->cqhd', weights, value_rows, preferred_element_type...  15.5 us
  transfers between devices with their start and end apart: 2, of which 0 were waited for; matrix products, arithmetic and copies ran while one was open for 3% of the time, Pallas kernels for 0%

commit v1 on v0

v1 whole, which is shorter than its diff:
```python
import functools

import jax
import jax.numpy as jnp
import numpy as np
from jax import lax
from jax.experimental import pallas as pl
from jax.experimental.pallas import tpu as pltpu
from jax.sharding import PartitionSpec as P

HEADS = 16
HEAD_DIM = 128
RING_Y, RING_Z, CORES = 4, 8, 2
Y_CAPS = (24, 17)
Z_CAPS = (12, 12, 11, 10)


def key_of(y, z, c):
    return (y * RING_Z + z) * CORES + c


def place():
    k = lax.axis_index("keys")
    return k // (RING_Z * CORES), (k // CORES) % RING_Z, k % CORES


def shifted(dy, dz, dc):
    pairs = []
    for y in range(RING_Y):
        for z in range(RING_Z):
            for c in range(CORES):
                to = key_of((y + dy) % RING_Y, (z + dz) % RING_Z, (c + dc) % CORES)
                pairs.append((key_of(y, z, c), to))
    return pairs


def greet(peers):
    barrier = pltpu.get_barrier_semaphore()
    for peer in peers:
        pl.semaphore_signal(
            barrier, inc=1, device_id={"keys": peer}, device_id_type=pl.DeviceIdType.MESH
        )
    pl.semaphore_wait(barrier, len(peers))


def peer_groups():
    y, z, c = place()
    core = [key_of(y, z, 1 - c)]
    depth = [key_of(y, (z + d) % RING_Z, c) for d in range(1, RING_Z)]
    row = [key_of((y + d) % RING_Y, z, c) for d in range(1, RING_Y)]
    return core, depth, row


def send(src, dst, send_sem, recv_sem, peer):
    copy = pltpu.make_async_remote_copy(
        src_ref=src,
        dst_ref=dst,
        send_sem=send_sem,
        recv_sem=recv_sem,
        device_id={"keys": peer},
        device_id_type=pl.DeviceIdType.MESH,
    )
    copy.start()
    return copy


def gather_ids_kernel(ids_ref, out_ref, held, send_sem, recv_sem):
    y, z, c = place()
    core, depth, row = peer_groups()
    greet(core + depth + row)
    held[y, z, c] = ids_ref[...]
    copies = [send(held.at[y, z, c], held.at[y, z, c], send_sem.at[0], recv_sem.at[0], core[0])]
    for copy in copies:
        copy.wait()
    copies = []
    for i, peer in enumerate(depth):
        copies.append(
            send(held.at[y, z], held.at[y, z], send_sem.at[1 + i], recv_sem.at[1 + i], peer)
        )
    for copy in copies:
        copy.wait()
    copies = []
    for i, peer in enumerate(row):
        copies.append(send(held.at[y], held.at[y], send_sem.at[8 + i], recv_sem.at[8 + i], peer))
    for copy in copies:
        copy.wait()
    out_ref[...] = held[...]


def gather_ids(ids):
    tile = jnp.zeros((8, 128), jnp.int32).at[0, : ids.size].set(ids.reshape(-1))
    shape = (RING_Y, RING_Z, CORES, 8, 128)
    held = pl.pallas_call(
        gather_ids_kernel,
        out_shape=jax.ShapeDtypeStruct(shape, jnp.int32),
        in_specs=[pl.BlockSpec(memory_space=pltpu.VMEM)],
        out_specs=pl.BlockSpec(memory_space=pltpu.VMEM),
        scratch_shapes=[
            pltpu.VMEM(shape, jnp.int32),
            pltpu.SemaphoreType.DMA((11,)),
            pltpu.SemaphoreType.DMA((11,)),
        ],
        compiler_params=pltpu.CompilerParams(collective_id=0, has_side_effects=True),
        name="gather_ids",
    )(tile)
    return held[..., 0, : ids.size].reshape(-1)


def merge(a, b):
    high = jnp.maximum(a[0:1], b[0:1])
    low = jnp.maximum(jnp.minimum(a[0:1], b[0:1]), jnp.maximum(a[1:2], b[1:2]))
    return jnp.concatenate([high, low, jnp.zeros((6, high.shape[1]), high.dtype)], axis=0)


def best_kernel(slab_ref, queries_ref, out_ref, own, after_core, after_depth, landed, send_sem, recv_sem):
    core, depth, row = peer_groups()
    greet(core + depth + row)
    scores = lax.dot_general(
        slab_ref[...],
        queries_ref[...],
        (((1,), (1,)), ((), ())),
        preferred_element_type=jnp.float32,
    )
    top = jnp.max(scores, axis=0, keepdims=True)
    at_top = scores == top
    ties = jnp.sum(jnp.where(at_top, 1.0, 0.0), axis=0, keepdims=True)
    rest = jnp.max(jnp.where(at_top, -jnp.inf, scores), axis=0, keepdims=True)
    second = jnp.where(ties > 1.5, top, rest)
    own[...] = jnp.concatenate([top, second, jnp.zeros((6, top.shape[1]), top.dtype)], axis=0)
    slot = 0
    holders = [own, after_core, after_depth, out_ref]
    for stage, peers in enumerate((core, depth, row)):
        source = holders[stage]
        copies = []
        for i, peer in enumerate(peers):
            copies.append(
                send(source, landed.at[slot + i], send_sem.at[slot + i], recv_sem.at[slot + i], peer)
            )
        for copy in copies:
            copy.wait()
        total = source[...]
        for i in range(len(peers)):
            total = merge(total, landed[slot + i])
        holders[stage + 1][...] = total
        slot += len(peers)


def best_two(key_slab, queries):
    rows = queries.shape[0]
    return pl.pallas_call(
        best_kernel,
        out_shape=jax.ShapeDtypeStruct((8, rows), jnp.float32),
        in_specs=[pl.BlockSpec(memory_space=pltpu.VMEM)] * 2,
        out_specs=pl.BlockSpec(memory_space=pltpu.VMEM),
        scratch_shapes=[pltpu.VMEM((8, rows), jnp.float32)] * 3
        + [
            pltpu.VMEM((11, 8, rows), jnp.float32),
            pltpu.SemaphoreType.DMA((11,)),
            pltpu.SemaphoreType.DMA((11,)),
        ],
        compiler_params=pltpu.CompilerParams(collective_id=1, has_side_effects=True),
        name="best_two",
    )(key_slab, queries)


def take_kernel(counts, reach, locs_ref, *refs):
    sources = refs[: len(counts)]
    outs = refs[len(counts) : -1]
    sems = refs[-1]
    starts = np.concatenate([[0], np.cumsum(counts)]).tolist()
    width = outs[0].shape[0]

    def begin(s, carry):
        for d, out in enumerate(outs):
            at = locs_ref[d, s]
            for k, source in enumerate(sources):
                if k not in reach[d]:
                    continue

                @pl.when((at >= starts[k]) & (at < starts[k + 1]))
                def _():
                    pltpu.make_async_copy(
                        source.at[at - starts[k]], out.at[s], sems.at[d, s]
                    ).start()

        return carry

    lax.fori_loop(0, width, begin, 0)

    def finish(s, carry):
        for d, out in enumerate(outs):
            pltpu.make_async_copy(sources[0].at[0], out.at[s], sems.at[d, s]).wait()
        return carry

    lax.fori_loop(0, width, finish, 0)


def take(sources, reach, locs):
    counts = tuple(s.shape[0] for s in sources)
    width = locs.shape[1]
    item = sources[0].shape[1:]
    nbytes = 4 * width * item[0] * item[1] * 2
    return pl.pallas_call(
        functools.partial(take_kernel, counts, reach),
        out_shape=[jax.ShapeDtypeStruct((width, *item), sources[0].dtype)] * 2,
        in_specs=[pl.BlockSpec(memory_space=pltpu.SMEM)]
        + [pl.BlockSpec(memory_space=pl.ANY)] * len(sources),
        out_specs=[pl.BlockSpec(memory_space=pl.ANY)] * 2,
        scratch_shapes=[pltpu.SemaphoreType.DMA((2, width))],
        cost_estimate=pl.CostEstimate(flops=0, bytes_accessed=nbytes, transcendentals=0),
        name="take_spans",
    )(locs, *sources)


def routes(all_ids):
    requests = all_ids.shape[0]
    per_device = requests // (RING_Y * RING_Z * CORES)
    index = np.arange(requests)
    k, n = index // per_device, index % per_device
    to_y, to_z = k // (RING_Z * CORES), (k // CORES) % RING_Z
    tie_y = jnp.asarray((n // 2 + k) % 2 == 1)
    tie_z = jnp.asarray((n + k) % 2 == 1)
    order = jnp.asarray(index, jnp.int32)
    to_y, to_z = jnp.asarray(to_y, jnp.int32), jnp.asarray(to_z, jnp.int32)
    y, z, c = place()
    shard, offset = all_ids // 64, all_ids % 64
    from_y, from_z, from_c = shard // (RING_Z * CORES), (shard // CORES) % RING_Z, shard % CORES
    loc = jnp.where(from_c == c, 0, 64) + offset
    base = 128
    sends = []

    def travel(position, target, ring, tie, node_of, mine, caps, loc, base):
        ahead = (target - position) % ring
        back = (ahead > ring // 2) | ((ahead == ring // 2) & tie)
        left = jnp.where(back, (ring - ahead) % ring, ahead)
        step = jnp.where(back, ring - 1, 1)
        way = back.astype(jnp.int32)
        for width in caps:
            node = node_of(position) * 2 + way
            moving = left > 0
            seat = jnp.where(moving, node, -1)
            priority = (16 - left) * 1024 + order
            before = (seat[:, None] == seat[None, :]) & (priority[:, None] < priority[None, :])
            rank = jnp.sum(before.astype(jnp.int32), axis=0)
            goes = moving & (rank < width)
            seat_rank = jnp.where(goes, node * 64 + rank, -1)
            wanted = (mine * 2 + np.arange(2, dtype=np.int32))[:, None] * 64 + np.arange(
                width, dtype=np.int32
            )
            hit = seat_rank[None, None, :] == wanted[:, :, None]
            sends.append(jnp.sum(jnp.where(hit, loc[None, None, :], 0), axis=-1))
            loc = jnp.where(goes, base + way * width + rank, loc)
            base += 2 * width
            position = jnp.where(goes, (position + step) % ring, position)
            left = left - goes.astype(jnp.int32)
        return jnp.max(left), loc, base

    stuck_y, loc, base = travel(
        from_y, to_y, RING_Y, tie_y, lambda p: p * RING_Z + from_z, y * RING_Z + z, Y_CAPS, loc, base
    )
    stuck_z, loc, base = travel(
        from_z, to_z, RING_Z, tie_z, lambda p: to_y * RING_Z + p, y * RING_Z + z, Z_CAPS, loc, base
    )
    table = loc.reshape(RING_Y * RING_Z, CORES, per_device)
    here = lax.dynamic_index_in_dim(table, y * RING_Z + z, 0, False)
    own = lax.dynamic_index_in_dim(here, c, 0, False)
    other = lax.dynamic_index_in_dim(here, 1 - c, 0, False)
    return sends, jnp.stack([own, other]), jnp.maximum(stuck_y, stuck_z)


def carried(held, sends, final, step):
    held_locs = lambda locs: jnp.where(locs < 128, locs + step, locs)
    sources = [held]
    y_count = 2 * len(Y_CAPS)
    moves = [(1, 0)] * len(Y_CAPS) + [(0, 1)] * len(Z_CAPS)
    for r, (dy, dz) in enumerate(moves):
        if dy:
            reach = [[0] + list(range(1 + d, len(sources), 2)) for d in range(2)]
        else:
            reach = [
                list(range(1 + y_count)) + list(range(1 + y_count + d, len(sources), 2))
                for d in range(2)
            ]
        up, down = take(sources, reach, held_locs(sends[r]))
        sources += [
            lax.ppermute(up, "keys", shifted(dy, dz, 0)),
            lax.ppermute(down, "keys", shifted(-dy, -dz, 0)),
        ]
    everything = list(range(len(sources)))
    own, other = take(sources, [everything] * 2, held_locs(final))
    return own, lax.ppermute(other, "keys", shifted(0, 0, 1))


def direct(neighbour_store, neighbour_ids):
    key_count = lax.axis_size("keys")
    shard_spans = neighbour_store.shape[0]
    flat_ids = neighbour_ids.reshape(-1)
    target, offset = flat_ids // shard_spans, flat_ids % shard_spans
    hit = target[:, None] == jnp.arange(key_count, dtype=jnp.int32)[None, :]
    table = jnp.sum(jnp.where(hit, offset[:, None], 0), axis=0)
    incoming = lax.all_to_all(table, "keys", split_axis=0, concat_axis=0, tiled=True)
    firsts, seconds = take([neighbour_store], [[0]] * 2, jnp.stack([incoming, incoming + 1]))
    arrived = [
        lax.all_to_all(spans, "keys", split_axis=0, concat_axis=0, tiled=True)
        for spans in (firsts, seconds)
    ]
    return take(arrived, [[0], [1]], jnp.stack([target, key_count + target]))


def body(span_queries, key_slab, neighbour_store, neighbour_ids, attn_queries, kv_weight):
    position = lax.axis_index("keys")
    y, z, c = place()
    own_spans = neighbour_ids.shape[0]
    span_rows = neighbour_store.shape[1]
    enc_width = neighbour_store.shape[2]
    half = span_rows // 2
    all_ids = gather_ids(neighbour_ids)
    kept = lax.dynamic_slice_in_dim(neighbour_store, c * half, half, axis=1)
    given = lax.dynamic_slice_in_dim(neighbour_store, (1 - c) * half, half, axis=1)
    held = jnp.concatenate([kept, lax.ppermute(given, "keys", shifted(0, 0, 1))], axis=0)
    groups = [[key_of(a, b, d) for a in range(RING_Y) for b in range(RING_Z)] for d in range(CORES)]
    weight_own = lax.all_gather(kv_weight, "keys", axis=1, axis_index_groups=groups)
    weight_other = lax.ppermute(weight_own, "keys", shifted(0, 0, 1))
    first = jnp.where(c == 0, weight_own, weight_other)
    second = jnp.where(c == 0, weight_other, weight_own)
    weights_all = jnp.stack([first, second], axis=2).reshape(2, HEADS * HEAD_DIM, enc_width)
    all_queries = lax.all_gather(span_queries, "keys", axis=0, tiled=True)
    sends, final, stuck = routes(all_ids)
    flag = jnp.full((8, 128), stuck, jnp.int32)
    seq = lax.axis_size("seq")
    worst = flag
    for d in range(1, seq):
        worst = jnp.maximum(
            worst, lax.ppermute(flag, "seq", [(s, (s + d) % seq) for s in range(seq)])
        )
    pieces = carried(held, sends, final, 0) + carried(held, sends, final, 1)

    def resend(store, ids, *fast):
        return tuple(
            spans[:, h * half : (h + 1) * half] for spans in direct(store, ids) for h in range(2)
        )

    pieces = lax.cond(
        worst[0, 0] > 0, resend, lambda store, ids, *fast: fast, neighbour_store, neighbour_ids, *pieces
    )
    neighbours = jnp.stack(
        [p.reshape(own_spans, 2, half, enc_width) for p in pieces], axis=1
    ).reshape(own_spans * 4 * span_rows, enc_width)
    best = best_two(key_slab, all_queries)
    best_scores = lax.dynamic_slice_in_dim(best, position * own_spans, own_spans, axis=1)[:2].T
    keys_values = jnp.einsum(
        "re,tce->rtc", neighbours, weights_all, preferred_element_type=jnp.float32
    ).astype(jnp.bfloat16)
    key_rows = keys_values[:, 0].reshape(own_spans, 4 * span_rows, HEADS, HEAD_DIM)
    value_rows = keys_values[:, 1].reshape(own_spans, 4 * span_rows, HEADS, HEAD_DIM)
    queries = attn_queries.reshape(own_spans, span_rows, HEADS, HEAD_DIM)
    logits = jnp.einsum(
        "cqhd,ckhd->chqk", queries, key_rows, preferred_element_type=jnp.float32
    ) * HEAD_DIM ** (-0.5)
    largest = jnp.max(logits, axis=-1, keepdims=True)
    expo_terms = jnp.exp(logits - largest)
    weights = (expo_terms / jnp.sum(expo_terms, axis=-1, keepdims=True)).astype(jnp.bfloat16)
    output = jnp.einsum("chqk,ckhd->cqhd", weights, value_rows, preferred_element_type=jnp.float32)
    attended = output.astype(jnp.bfloat16).reshape(own_spans * span_rows, HEADS * HEAD_DIM)
    return (best_scores, attended)


def solution(mesh):
    return jax.shard_map(
        body,
        mesh=mesh,
        in_specs=(
            P(("keys", "seq"), None),
            P("keys", None),
            P("keys", None, None),
            P(("keys", "seq"), None),
            P(("keys", "seq"), None),
            P(None, "keys", None),
        ),
        out_specs=(P(("keys", "seq"), None), P(("keys", "seq"), None)),
        check_vma=False,
    )
```

time: 607 us -> 974 us (1.60)
  Pallas kernels: 0 us -> 723 us
  blocking collectives: 495 us -> 47.7 us
  starting transfers between devices: 6.45 us -> 64.4 us
  other arithmetic: 10.8 us -> 27.6 us
    pallas_call x0 -> x16, Pallas kernels: none -> 723 us  [the longest x14 689 us: take(): pl.pallas_call(functools.partial(take_kernel, counts, reach), out_shape=[...]
    all_gather x3 -> x1, blocking collectives: 473 us -> 47.7 us  [body(): all_queries = lax.all_gather(span_queries, 'keys', axis=0, tiled=True)]
    ppermute x0 -> x31, starting transfers between devices: none -> 64.4 us  [the longest x12 44.5 us: carried(): lax.ppermute(down, 'keys', shifted(-dy, -dz, 0))]
    all_to_all x1 -> x0, blocking collectives: 22.2 us -> none  [body(): lax.all_to_all(table, 'keys', split_axis=0, concat_axis=0, tiled=True)]
    gather x2 -> x0, local copies, waits for them, and re-layouts: 18.1 us -> none  [the longest x1 11.8 us: body(): outgoing = neighbour_store[incoming]]
    unnamed x17 -> x79, local copies, waits for them, and re-layouts: 16.8 us -> 34.4 us
  transfers between devices with their start and end apart: 2 -> 32, of which waited for: 0 -> 0; matrix products, arithmetic and copies ran while one was open for 3% -> 3% of each run, Pallas kernels for 0% -> 75%
where the time goes in v1:
time: 974 us; the launch traced here: 965 us
  Pallas kernels  723 us (74%)
  starting transfers between devices  64.4 us (7%)
  blocking collectives  47.7 us (5%)
  local copies, waits for them, and re-layouts  46.8 us (5%)
  matrix products  37.8 us (4%)
  other arithmetic  27.6 us (3%)
  between operations  17.1 us (2%)
    pallas_call x14, Pallas kernels, take(): pl.pallas_call(functools.partial(take_kernel, counts, reach), out_shape=[...  689 us
    all_gather x1, blocking collectives, body(): all_queries = lax.all_gather(span_queries, 'keys', axis=0, tiled=True)  47.7 us
    ppermute x12, starting transfers between devices, carried(): lax.ppermute(down, 'keys', shifted(-dy, -dz, 0))  44.5 us
    unnamed x79, local copies, waits for them, and re-layouts  34.4 us
  transfers between devices with their start and end apart: 32, of which 0 were waited for; matrix products, arithmetic and copies ran while one was open for 3% of the time, Pallas kernels for 75%

profile of v1, /device:TPU:1, one launch (start us, length us, event | category | flops | bytes accessed | tf_op | source)
XLA Modules:
  0.0 964.9 jit_solution(13317401214996491038)
XLA Ops:
  8.0 6.8 constant_dynamic-slice_fusion.1
  14.8 3.2 collective-permute-start.3
  18.8 18.3 %gather_ids.1 = s32[4,8,2,8,128]{4,3,2,1,0:T(8,128)} custom-call(s32[8,128]{1,0:T(8,128)} %scatter.4.ids_ref), custom_call_target="tpu_custom_call" | custom-call | tf_op jit(solution)/shard_map/gather_ids/pallas_call | solution.py:93
  43.0 6.8 pad_maximum_fusion.refs_0_
  49.8 85.6 %take_spans.25 = (bf16[24,32,896]{2,1,0:T(8,128)(2,1)}, bf16[24,32,896]{2,1,0:T(8,128)(2,1)}) custom-call(s32[2,24]{1,0:T(2,128)} %compare_select_fusion.16.locs_ref, bf16[128,32,896]{2,1,0:T(8,128)(2,1)} %pad_maximum_fusion.refs_0_), custom_call_target="tpu_custom_call" | custom-call | bytes 5505024 | tf_op jit(solution)/shard_map/take_spans/pallas_call | solution.py:203
  135.5 2.7 collective-permute-start.18
  138.2 85.6 %take_spans.18 = (bf16[24,32,896]{2,1,0:T(8,128)(2,1)}, bf16[24,32,896]{2,1,0:T(8,128)(2,1)}) custom-call(s32[2,24]{1,0:T(2,128)} %copy-done.31, bf16[128,32,896]{2,1,0:T(8,128)(2,1)} %pad_maximum_fusion.refs_0_), custom_call_target="tpu_custom_call" | custom-call | bytes 5505024 | tf_op jit(solution)/shard_map/take_spans/pallas_call | solution.py:203
  223.9 2.7 collective-permute-start.5
  227.7 61.2 %take_spans.26 = (bf16[17,32,896]{2,1,0:T(8,128)(2,1)}, bf16[17,32,896]{2,1,0:T(8,128)(2,1)}) custom-call(s32[2,17]{1,0:T(2,128)} %compare_select_fusion.15.locs_ref, bf16[128,32,896]{2,1,0:T(8,128)(2,1)} %pad_maximum_fusion.refs_0_, bf16[24,32,896]{2,1,0:T(8,128)(2,1)} %collective-permute-done.17.refs_1_, bf16[24,32,896]{2,1,0:T(8,128)(2,1)} %collective-permute-done.18.refs_2_), custom_call_target="tpu_custom_call" | custom-call | bytes 3899392 | tf_op jit(solution)/shard_map/take_spans/pallas_call | solution.py:203
  288.9 2.7 collective-permute-start.20
  293.8 61.2 %take_spans.19 = (bf16[17,32,896]{2,1,0:T(8,128)(2,1)}, bf16[17,32,896]{2,1,0:T(8,128)(2,1)}) custom-call(s32[2,17]{1,0:T(2,128)} %copy-done.32, bf16[128,32,896]{2,1,0:T(8,128)(2,1)} %pad_maximum_fusion.refs_0_, bf16[24,32,896]{2,1,0:T(8,128)(2,1)} %copy-done, bf16[24,32,896]{2,1,0:T(8,128)(2,1)} %copy-done.1), custom_call_target="tpu_custom_call" | custom-call | bytes 3899392 | tf_op jit(solution)/shard_map/take_spans/pallas_call | solution.py:203
  355.1 2.9 collective-permute-start.7
  359.2 43.7 %take_spans.27 = (bf16[12,32,896]{2,1,0:T(8,128)(2,1)}, bf16[12,32,896]{2,1,0:T(8,128)(2,1)}) custom-call(s32[2,12]{1,0:T(2,128)} %compare_select_fusion.14.locs_ref, bf16[128,32,896]{2,1,0:T(8,128)(2,1)} %pad_maximum_fusion.refs_0_, bf16[24,32,896]{2,1,0:T(8,128)(2,1)} %collective-permute-done.17.refs_1_, ...), custom_call_target="tpu_custom_call" | custom-call | bytes 2752512 | tf_op jit(solution)/shard_map/take_spans/pallas_call | solution.py:203
  403.8 2.0 collective-permute-start.22
  407.7 43.7 %take_spans.20 = (bf16[12,32,896]{2,1,0:T(8,128)(2,1)}, bf16[12,32,896]{2,1,0:T(8,128)(2,1)}) custom-call(s32[2,12]{1,0:T(2,128)} %copy-done.27, bf16[128,32,896]{2,1,0:T(8,128)(2,1)} %pad_maximum_fusion.refs_0_, bf16[24,32,896]{2,1,0:T(8,128)(2,1)} %copy-done, bf16[24,32,896]{2,1,0:T(8,128)(2,1)} %copy-done.1, bf16[17,32,896]{2,1,0:T(8,128)(2,1)} %copy-done.2, ...), custom_call_target="tpu_custom_call" | custom-call | bytes 2752512 | tf_op jit(solution)/shard_map/take_spans/pallas_call | solution.py:203
  451.5 2.7 collective-permute-start.9
  454.1 5.7 collective-permute-start.30
  462.2 43.7 %take_spans.28 = (bf16[12,32,896]{2,1,0:T(8,128)(2,1)}, bf16[12,32,896]{2,1,0:T(8,128)(2,1)}) custom-call(s32[2,12]{1,0:T(2,128)} %compare_select_fusion.13.locs_ref, bf16[128,32,896]{2,1,0:T(8,128)(2,1)} %pad_maximum_fusion.refs_0_, bf16[24,32,896]{2,1,0:T(8,128)(2,1)} %collective-permute-done.17.refs_1_, ...), custom_call_target="tpu_custom_call" | custom-call | bytes 2752512 | tf_op jit(solution)/shard_map/take_spans/pallas_call | solution.py:203
  506.1 2.7 collective-permute-start.24
  510.4 43.7 %take_spans.21 = (bf16[12,32,896]{2,1,0:T(8,128)(2,1)}, bf16[12,32,896]{2,1,0:T(8,128)(2,1)}) custom-call(s32[2,12]{1,0:T(2,128)} %copy-done.30, bf16[128,32,896]{2,1,0:T(8,128)(2,1)} %pad_maximum_fusion.refs_0_, bf16[24,32,896]{2,1,0:T(8,128)(2,1)} %copy-done, bf16[24,32,896]{2,1,0:T(8,128)(2,1)} %copy-done.1, bf16[17,32,896]{2,1,0:T(8,128)(2,1)} %copy-done.2, ...), custom_call_target="tpu_custom_call" | custom-call | bytes 2752512 | tf_op jit(solution)/shard_map/take_spans/pallas_call | solution.py:203
  554.2 2.7 collective-permute-start.11
  559.7 40.2 %take_spans.29 = (bf16[11,32,896]{2,1,0:T(8,128)(2,1)}, bf16[11,32,896]{2,1,0:T(8,128)(2,1)}) custom-call(s32[2,11]{1,0:T(2,128)} %compare_select_fusion.12.locs_ref, bf16[128,32,896]{2,1,0:T(8,128)(2,1)} %pad_maximum_fusion.refs_0_, bf16[24,32,896]{2,1,0:T(8,128)(2,1)} %collective-permute-done.17.refs_1_, ...), custom_call_target="tpu_custom_call" | custom-call | bytes 2523136 | tf_op jit(solution)/shard_map/take_spans/pallas_call | solution.py:203
  600.0 2.7 collective-permute-start.26
  604.4 40.2 %take_spans.22 = (bf16[11,32,896]{2,1,0:T(8,128)(2,1)}, bf16[11,32,896]{2,1,0:T(8,128)(2,1)}) custom-call(s32[2,11]{1,0:T(2,128)} %copy-done.28, bf16[128,32,896]{2,1,0:T(8,128)(2,1)} %pad_maximum_fusion.refs_0_, bf16[24,32,896]{2,1,0:T(8,128)(2,1)} %copy-done, bf16[24,32,896]{2,1,0:T(8,128)(2,1)} %copy-done.1, bf16[17,32,896]{2,1,0:T(8,128)(2,1)} %copy-done.2, ...), custom_call_target="tpu_custom_call" | custom-call | bytes 2523136 | tf_op jit(solution)/shard_map/take_spans/pallas_call | solution.py:203
  644.8 2.7 collective-permute-start.13
  650.1 36.7 %take_spans.30 = (bf16[10,32,896]{2,1,0:T(8,128)(2,1)}, bf16[10,32,896]{2,1,0:T(8,128)(2,1)}) custom-call(s32[2,10]{1,0:T(2,128)} %compare_select_fusion.11.locs_ref, bf16[128,32,896]{2,1,0:T(8,128)(2,1)} %pad_maximum_fusion.refs_0_, bf16[24,32,896]{2,1,0:T(8,128)(2,1)} %collective-permute-done.17.refs_1_, ...), custom_call_target="tpu_custom_call" | custom-call | bytes 2293760 | tf_op jit(solution)/shard_map/take_spans/pallas_call | solution.py:203
  687.0 15.7 %collective-permute-start.28 = (bf16[10,32,896]{2,1,0:T(8,128)(2,1)}, bf16[10,32,896]{2,1,0:T(8,128)(2,1)S(1)}, u32[]{:S(2)}, u32[]{:S(2)}) collective-permute-start(bf16[10,32,896]{2,1,0:T(8,128)(2,1)} %get-tuple-element.113), channel_id=1, source_target_pairs={{0,56},{4,60},{8,0},{12,4},{16,8},{20,12},{24,16},{28,20},{32,24},... | collective-permute-start | bytes 1720328 | tf_op jit(solution)/shard_map/ppermute | solution.py:287
  704.3 36.7 %take_spans.23 = (bf16[10,32,896]{2,1,0:T(8,128)(2,1)}, bf16[10,32,896]{2,1,0:T(8,128)(2,1)}) custom-call(s32[2,10]{1,0:T(2,128)} %copy-done.29, bf16[128,32,896]{2,1,0:T(8,128)(2,1)} %pad_maximum_fusion.refs_0_, bf16[24,32,896]{2,1,0:T(8,128)(2,1)} %copy-done, bf16[24,32,896]{2,1,0:T(8,128)(2,1)} %copy-done.1, bf16[17,32,896]{2,1,0:T(8,128)(2,1)} %copy-done.2, ...), custom_call_target="tpu_custom_call" | custom-call | bytes 2293760 | tf_op jit(solution)/shard_map/take_spans/pallas_call | solution.py:203
  741.2 2.7 collective-permute-start.15
  747.8 2.5 collective-permute-start.1
  750.3 22.9 %take_spans.31 = (bf16[12,32,896]{2,1,0:T(8,128)(2,1)S(1)}, bf16[12,32,896]{2,1,0:T(8,128)(2,1)}) custom-call(s32[2,12]{1,0:T(2,128)} %get-tuple-element.205.locs_ref, bf16[128,32,896]{2,1,0:T(8,128)(2,1)} %pad_maximum_fusion.refs_0_, bf16[24,32,896]{2,1,0:T(8,128)(2,1)} %collective-permute-done.17.refs_1_, ...), custom_call_target="tpu_custom_call" | custom-call | bytes 2752512 | tf_op jit(solution)/shard_map/take_spans/pallas_call | solution.py:203
  773.3 4.0 collective-permute-start.29
  778.1 43.9 %take_spans.24 = (bf16[12,32,896]{2,1,0:T(8,128)(2,1)}, bf16[12,32,896]{2,1,0:T(8,128)(2,1)}) custom-call(s32[2,12]{1,0:T(2,128)} %get-tuple-element.206.locs_ref, bf16[128,32,896]{2,1,0:T(8,128)(2,1)} %pad_maximum_fusion.refs_0_, bf16[24,32,896]{2,1,0:T(8,128)(2,1)} %copy-done, bf16[24,32,896]{2,1,0:T(8,128)(2,1)} %copy-done.1, ...), custom_call_target="tpu_custom_call" | custom-call | bytes 2752512 | tf_op jit(solution)/shard_map/take_spans/pallas_call | solution.py:203
  822.2 47.7 %all-gather.1 = bf16[64,6,768]{2,1,0:T(8,128)(2,1)S(1)} all-gather(bf16[1,6,768]{2,1,0:T(8,128)(2,1)S(1)} %bitcast.87), channel_id=1, replica_groups=mesh['keys'=64,'seq'=4] {'keys'}, dimensions={0}, use_global_device_ids=true | all-gather | bytes 599040 | tf_op jit(solution)/shard_map/all_gather | solution.py:327
  870.9 15.2 %best_two.1 = f32[8,384]{1,0:T(8,128)} custom-call(bf16[64,768]{1,0:T(8,128)(2,1)} %slab_ref.1, bf16[384,768]{1,0:T(8,128)(2,1)} %reshape.487.queries_ref), custom_call_target="tpu_custom_call" | custom-call | tf_op jit(solution)/shard_map/best_two/pallas_call | solution.py:150
  888.7 1.6 copy.88
  891.6 1.7 pad_maximum_fusion.2
  893.6 1.7 copy-done.13
  895.3 2.7 select_bitcast_fusion.1
  898.1 3.6 pad_maximum_fusion.1
  901.7 18.7 %convolution_convert_fusion = bf16[1536,2,2048]{2,0,1:T(8,128)(2,1)} fusion(bf16[1536,896,1]{1,0,2:T(8,128)(2,1)S(1)} %bitcast.80, bf16[2,2048,896]{2,1,0:T(8,128)(2,1)} %bitcast.74), kind=kOutput, calls=%fused_computation.16 | convolution fusion | flops 11280580608 | bytes 22675456 | tf_op jit(solution)/shard_map/re,tce->rtc/dot_general | solution.py:351
  920.4 5.5 slice_bitcast_fusion.1
  925.9 2.3 copy.87
  928.3 3.7 fusion.5
  932.0 2.4 fusion.84
  934.7 5.0 copy.89
  939.7 15.4 %fusion.16 = bf16[6,64,16,128]{3,1,2,0:T(8,128)(2,1)S(1)} fusion(bf16[6,256,16,128]{3,2,1,0:T(8,128)(2,1)} %bitcast.75, f32[6,16,64]{2,1,0:T(8,128)S(1)} %fusion.84, f32[6,16,256,64]{2,3,1,0:T(8,128)} %copy-done.8), kind=kOutput, calls=%fused_computation.45 | convolution fusion | flops 411310336 | bytes 14180352 | tf_op jit(solution)/shard_map/chqk,ckhd->cqhd/dot_general | solution.py:363
  956.1 1.6 copy.102
  (176 shorter events, 38.0 us)
Async XLA Ops:
  7.2 447.0 %all-gather.4.cloned.1.call-start = ((), (), s32[]{:S(2)}) async-start(), calls=%async_computation.3 | async-start | bytes 3784704 | tf_op jit(solution)/shard_map/all_gather | solution.py:322
  7.9 10.1 %copy-start.34 = (s32[6,2]{0,1:T(2,128)S(1)}, s32[6,2]{0,1:T(2,128)}, u32[]{:S(2)}) copy-start(s32[6,2]{0,1:T(2,128)} %param.30) | copy-start | bytes 148
  7.9 30.4 %copy-start.23 = (s32[768]{0:T(1024)S(1)}, s32[768]{0:T(1024)}, u32[]{:S(2)}) copy-start(s32[768]{0:T(1024)} %constant.351) | copy-start | bytes 9220
  7.9 30.4 %copy-start.33 = (s32[768]{0:T(1024)S(1)}, s32[768]{0:T(1024)}, u32[]{:S(2)}) copy-start(s32[768]{0:T(1024)} %constant.344.clone) | copy-start | bytes 9220
  8.0 30.4 %copy-start.35 = (pred[768]{0:T(1024)(128)(4,1)S(1)}, pred[768]{0:T(1024)(128)(4,1)}, u32[]{:S(2)}) copy-start(pred[768]{0:T(1024)(128)(4,1)} %constant.342.clone) | copy-start | bytes 2308
  8.0 30.9 %copy-start.24 = (s32[768]{0:T(1024)S(1)}, s32[768]{0:T(1024)}, u32[]{:S(2)}) copy-start(s32[768]{0:T(1024)} %constant.343.clone) | copy-start | bytes 9220
  8.0 30.9 %copy-start.25 = (pred[768]{0:T(1024)(128)(4,1)S(1)}, pred[768]{0:T(1024)(128)(4,1)}, u32[]{:S(2)}) copy-start(pred[768]{0:T(1024)(128)(4,1)} %constant.341.clone) | copy-start | bytes 2308
  14.8 28.2 %collective-permute-start.3 = (bf16[64,32,896]{2,1,0:T(8,128)(2,1)}, bf16[64,32,896]{2,1,0:T(8,128)(2,1)}, u32[]{:S(2)}, u32[]{:S(2)}) collective-permute-start(bf16[64,32,896]{2,1,0:T(8,128)(2,1)} %get-tuple-element.187), channel_id=1, source_target_pairs={{0,4},{4,0},{8,12},{12,8},{16,20},{20,16},{24,28},{28,24},{32,36},... | collective-permute-start | bytes 11010056 | tf_op jit(solution)/shard_map/ppermute | solution.py:320
  42.4 7.4 copy-start.31
  135.4 92.2 %collective-permute-start.17 = (bf16[24,32,896]{2,1,0:T(8,128)(2,1)}, bf16[24,32,896]{2,1,0:T(8,128)(2,1)}, u32[]{:S(2)}, u32[]{:S(2)}) collective-permute-start(bf16[24,32,896]{2,1,0:T(8,128)(2,1)} %get-tuple-element.102), channel_id=1, source_target_pairs={{0,64},{4,68},{8,72},{12,76},{16,80},{20,84},{24,88},{28,92},{32,9... | collective-permute-start | bytes 4128776 | tf_op jit(solution)/shard_map/ppermute | solution.py:286
  135.5 92.1 %collective-permute-start.18 = (bf16[24,32,896]{2,1,0:T(8,128)(2,1)}, bf16[24,32,896]{2,1,0:T(8,128)(2,1)}, u32[]{:S(2)}, u32[]{:S(2)}) collective-permute-start(bf16[24,32,896]{2,1,0:T(8,128)(2,1)} %get-tuple-element.103), channel_id=1, source_target_pairs={{0,192},{4,196},{8,200},{12,204},{16,208},{20,212},{24,216},{28,22... | collective-permute-start | bytes 4128776 | tf_op jit(solution)/shard_map/ppermute | solution.py:287
  223.8 67.8 %collective-permute-start.4 = (bf16[24,32,896]{2,1,0:T(8,128)(2,1)}, bf16[24,32,896]{2,1,0:T(8,128)(2,1)S(1)}, u32[]{:S(2)}, u32[]{:S(2)}) collective-permute-start(bf16[24,32,896]{2,1,0:T(8,128)(2,1)} %get-tuple-element.88), channel_id=1, source_target_pairs={{0,64},{4,68},{8,72},{12,76},{16,80},{20,84},{24,88},{28,92},{32,9... | collective-permute-start | bytes 4128776 | tf_op jit(solution)/shard_map/ppermute | solution.py:286
  223.9 67.7 %collective-permute-start.5 = (bf16[24,32,896]{2,1,0:T(8,128)(2,1)}, bf16[24,32,896]{2,1,0:T(8,128)(2,1)S(1)}, u32[]{:S(2)}, u32[]{:S(2)}) collective-permute-start(bf16[24,32,896]{2,1,0:T(8,128)(2,1)} %get-tuple-element.89), channel_id=1, source_target_pairs={{0,192},{4,196},{8,200},{12,204},{16,208},{20,212},{24,216},{28,22... | collective-permute-start | bytes 4128776 | tf_op jit(solution)/shard_map/ppermute | solution.py:287
  227.1 61.7 %copy-start.32 = (s32[2,17]{1,0:T(2,128)}, s32[2,17]{1,0:T(2,128)S(1)}, u32[]{:S(2)}) copy-start(s32[2,17]{1,0:T(2,128)S(1)} %copy.60.locs_ref) | copy-start | bytes 412
  288.8 70.4 %collective-permute-start.19 = (bf16[17,32,896]{2,1,0:T(8,128)(2,1)}, bf16[17,32,896]{2,1,0:T(8,128)(2,1)}, u32[]{:S(2)}, u32[]{:S(2)}) collective-permute-start(bf16[17,32,896]{2,1,0:T(8,128)(2,1)} %get-tuple-element.104), channel_id=1, source_target_pairs={{0,64},{4,68},{8,72},{12,76},{16,80},{20,84},{24,88},{28,92},{32,9... | collective-permute-start | bytes 2924552 | tf_op jit(solution)/shard_map/ppermute | solution.py:286
  288.9 70.3 %collective-permute-start.20 = (bf16[17,32,896]{2,1,0:T(8,128)(2,1)}, bf16[17,32,896]{2,1,0:T(8,128)(2,1)}, u32[]{:S(2)}, u32[]{:S(2)}) collective-permute-start(bf16[17,32,896]{2,1,0:T(8,128)(2,1)} %get-tuple-element.105), channel_id=1, source_target_pairs={{0,192},{4,196},{8,200},{12,204},{16,208},{20,212},{24,216},{28,22... | collective-permute-start | bytes 2924552 | tf_op jit(solution)/shard_map/ppermute | solution.py:287
  355.0 50.7 %collective-permute-start.6 = (bf16[17,32,896]{2,1,0:T(8,128)(2,1)}, bf16[17,32,896]{2,1,0:T(8,128)(2,1)S(1)}, u32[]{:S(2)}, u32[]{:S(2)}) collective-permute-start(bf16[17,32,896]{2,1,0:T(8,128)(2,1)} %get-tuple-element.90), channel_id=1, source_target_pairs={{0,64},{4,68},{8,72},{12,76},{16,80},{20,84},{24,88},{28,92},{32,9... | collective-permute-start | bytes 2924552 | tf_op jit(solution)/shard_map/ppermute | solution.py:286
  355.1 50.6 %collective-permute-start.7 = (bf16[17,32,896]{2,1,0:T(8,128)(2,1)}, bf16[17,32,896]{2,1,0:T(8,128)(2,1)S(1)}, u32[]{:S(2)}, u32[]{:S(2)}) collective-permute-start(bf16[17,32,896]{2,1,0:T(8,128)(2,1)} %get-tuple-element.91), channel_id=1, source_target_pairs={{0,192},{4,196},{8,200},{12,204},{16,208},{20,212},{24,216},{28,22... | collective-permute-start | bytes 2924552 | tf_op jit(solution)/shard_map/ppermute | solution.py:287
  358.7 44.3 %copy-start.27 = (s32[2,12]{1,0:T(2,128)}, s32[2,12]{1,0:T(2,128)S(1)}, u32[]{:S(2)}) copy-start(s32[2,12]{1,0:T(2,128)S(1)} %copy.61.locs_ref) | copy-start | bytes 292
  403.0 57.5 %collective-permute-start.21 = (bf16[12,32,896]{2,1,0:T(8,128)(2,1)}, bf16[12,32,896]{2,1,0:T(8,128)(2,1)S(1)}, u32[]{:S(2)}, u32[]{:S(2)}) collective-permute-start(bf16[12,32,896]{2,1,0:T(8,128)(2,1)} %get-tuple-element.106), channel_id=1, source_target_pairs={{0,8},{4,12},{8,16},{12,20},{16,24},{20,28},{24,32},{28,36},{32,40... | collective-permute-start | bytes 2064392 | tf_op jit(solution)/shard_map/ppermute | solution.py:286
  403.8 56.7 %collective-permute-start.22 = (bf16[12,32,896]{2,1,0:T(8,128)(2,1)}, bf16[12,32,896]{2,1,0:T(8,128)(2,1)S(1)}, u32[]{:S(2)}, u32[]{:S(2)}) collective-permute-start(bf16[12,32,896]{2,1,0:T(8,128)(2,1)} %get-tuple-element.107), channel_id=1, source_target_pairs={{0,56},{4,60},{8,0},{12,4},{16,8},{20,12},{24,16},{28,20},{32,24},... | collective-permute-start | bytes 2064392 | tf_op jit(solution)/shard_map/ppermute | solution.py:287
  451.4 57.3 %collective-permute-start.8 = (bf16[12,32,896]{2,1,0:T(8,128)(2,1)}, bf16[12,32,896]{2,1,0:T(8,128)(2,1)S(1)}, u32[]{:S(2)}, u32[]{:S(2)}) collective-permute-start(bf16[12,32,896]{2,1,0:T(8,128)(2,1)} %get-tuple-element.92), channel_id=1, source_target_pairs={{0,8},{4,12},{8,16},{12,20},{16,24},{20,28},{24,32},{28,36},{32,40... | collective-permute-start | bytes 2064392 | tf_op jit(solution)/shard_map/ppermute | solution.py:286
  451.5 57.2 %collective-permute-start.9 = (bf16[12,32,896]{2,1,0:T(8,128)(2,1)}, bf16[12,32,896]{2,1,0:T(8,128)(2,1)S(1)}, u32[]{:S(2)}, u32[]{:S(2)}) collective-permute-start(bf16[12,32,896]{2,1,0:T(8,128)(2,1)} %get-tuple-element.93), channel_id=1, source_target_pairs={{0,56},{4,60},{8,0},{12,4},{16,8},{20,12},{24,16},{28,20},{32,24},... | collective-permute-start | bytes 2064392 | tf_op jit(solution)/shard_map/ppermute | solution.py:287
  454.1 439.4 %collective-permute-start.30 = (bf16[2,32,32,896]{3,2,1,0:T(8,128)(2,1)}, bf16[2,32,32,896]{3,2,1,0:T(8,128)(2,1)}, u32[]{:S(2)}, u32[]{:S(2)}) collective-permute-start(bf16[2,32,32,896]{3,2,1,0:T(8,128)(2,1)} %bitcast.78), channel_id=1, source_target_pairs={{0,4},{4,0},{8,12},{12,8},{16,20},{20,16},{24,28},{28,24},{32,36},... | collective-permute-start | bytes 11010056 | tf_op jit(solution)/shard_map/ppermute | solution.py:323
  459.9 46.0 %copy-start.30 = (s32[2,12]{1,0:T(2,128)}, s32[2,12]{1,0:T(2,128)S(1)}, u32[]{:S(2)}) copy-start(s32[2,12]{1,0:T(2,128)S(1)} %copy.62.locs_ref) | copy-start | bytes 292
  506.0 52.0 %collective-permute-start.23 = (bf16[12,32,896]{2,1,0:T(8,128)(2,1)}, bf16[12,32,896]{2,1,0:T(8,128)(2,1)S(1)}, u32[]{:S(2)}, u32[]{:S(2)}) collective-permute-start(bf16[12,32,896]{2,1,0:T(8,128)(2,1)} %get-tuple-element.108), channel_id=1, source_target_pairs={{0,8},{4,12},{8,16},{12,20},{16,24},{20,28},{24,32},{28,36},{32,40... | collective-permute-start | bytes 2064392 | tf_op jit(solution)/shard_map/ppermute | solution.py:286
  506.1 51.9 %collective-permute-start.24 = (bf16[12,32,896]{2,1,0:T(8,128)(2,1)}, bf16[12,32,896]{2,1,0:T(8,128)(2,1)S(1)}, u32[]{:S(2)}, u32[]{:S(2)}) collective-permute-start(bf16[12,32,896]{2,1,0:T(8,128)(2,1)} %get-tuple-element.109), channel_id=1, source_target_pairs={{0,56},{4,60},{8,0},{12,4},{16,8},{20,12},{24,16},{28,20},{32,24},... | collective-permute-start | bytes 2064392 | tf_op jit(solution)/shard_map/ppermute | solution.py:287
  554.2 48.5 %collective-permute-start.10 = (bf16[12,32,896]{2,1,0:T(8,128)(2,1)}, bf16[12,32,896]{2,1,0:T(8,128)(2,1)S(1)}, u32[]{:S(2)}, u32[]{:S(2)}) collective-permute-start(bf16[12,32,896]{2,1,0:T(8,128)(2,1)} %get-tuple-element.94), channel_id=1, source_target_pairs={{0,8},{4,12},{8,16},{12,20},{16,24},{20,28},{24,32},{28,36},{32,40... | collective-permute-start | bytes 2064392 | tf_op jit(solution)/shard_map/ppermute | solution.py:286
  554.2 48.4 %collective-permute-start.11 = (bf16[12,32,896]{2,1,0:T(8,128)(2,1)}, bf16[12,32,896]{2,1,0:T(8,128)(2,1)S(1)}, u32[]{:S(2)}, u32[]{:S(2)}) collective-permute-start(bf16[12,32,896]{2,1,0:T(8,128)(2,1)} %get-tuple-element.95), channel_id=1, source_target_pairs={{0,56},{4,60},{8,0},{12,4},{16,8},{20,12},{24,16},{28,20},{32,24},... | collective-permute-start | bytes 2064392 | tf_op jit(solution)/shard_map/ppermute | solution.py:287
  557.4 42.6 %copy-start.28 = (s32[2,11]{1,0:T(2,128)}, s32[2,11]{1,0:T(2,128)S(1)}, u32[]{:S(2)}) copy-start(s32[2,11]{1,0:T(2,128)S(1)} %copy.63.locs_ref) | copy-start | bytes 268
  599.9 48.5 %collective-permute-start.25 = (bf16[11,32,896]{2,1,0:T(8,128)(2,1)}, bf16[11,32,896]{2,1,0:T(8,128)(2,1)S(1)}, u32[]{:S(2)}, u32[]{:S(2)}) collective-permute-start(bf16[11,32,896]{2,1,0:T(8,128)(2,1)} %get-tuple-element.110), channel_id=1, source_target_pairs={{0,8},{4,12},{8,16},{12,20},{16,24},{20,28},{24,32},{28,36},{32,40... | collective-permute-start | bytes 1892360 | tf_op jit(solution)/shard_map/ppermute | solution.py:286
  600.0 48.4 %collective-permute-start.26 = (bf16[11,32,896]{2,1,0:T(8,128)(2,1)}, bf16[11,32,896]{2,1,0:T(8,128)(2,1)S(1)}, u32[]{:S(2)}, u32[]{:S(2)}) collective-permute-start(bf16[11,32,896]{2,1,0:T(8,128)(2,1)} %get-tuple-element.111), channel_id=1, source_target_pairs={{0,56},{4,60},{8,0},{12,4},{16,8},{20,12},{24,16},{28,20},{32,24},... | collective-permute-start | bytes 1892360 | tf_op jit(solution)/shard_map/ppermute | solution.py:287
  644.7 58.0 %collective-permute-start.12 = (bf16[11,32,896]{2,1,0:T(8,128)(2,1)}, bf16[11,32,896]{2,1,0:T(8,128)(2,1)S(1)}, u32[]{:S(2)}, u32[]{:S(2)}) collective-permute-start(bf16[11,32,896]{2,1,0:T(8,128)(2,1)} %get-tuple-element.96), channel_id=1, source_target_pairs={{0,8},{4,12},{8,16},{12,20},{16,24},{20,28},{24,32},{28,36},{32,40... | collective-permute-start | bytes 1892360 | tf_op jit(solution)/shard_map/ppermute | solution.py:286
  644.8 57.9 %collective-permute-start.13 = (bf16[11,32,896]{2,1,0:T(8,128)(2,1)}, bf16[11,32,896]{2,1,0:T(8,128)(2,1)S(1)}, u32[]{:S(2)}, u32[]{:S(2)}) collective-permute-start(bf16[11,32,896]{2,1,0:T(8,128)(2,1)} %get-tuple-element.97), channel_id=1, source_target_pairs={{0,56},{4,60},{8,0},{12,4},{16,8},{20,12},{24,16},{28,20},{32,24},... | collective-permute-start | bytes 1892360 | tf_op jit(solution)/shard_map/ppermute | solution.py:287
  647.9 39.0 %copy-start.29 = (s32[2,10]{1,0:T(2,128)}, s32[2,10]{1,0:T(2,128)S(1)}, u32[]{:S(2)}) copy-start(s32[2,10]{1,0:T(2,128)S(1)} %copy.64.locs_ref) | copy-start | bytes 244
  686.9 59.7 %collective-permute-start.27 = (bf16[10,32,896]{2,1,0:T(8,128)(2,1)}, bf16[10,32,896]{2,1,0:T(8,128)(2,1)S(1)}, u32[]{:S(2)}, u32[]{:S(2)}) collective-permute-start(bf16[10,32,896]{2,1,0:T(8,128)(2,1)} %get-tuple-element.112), channel_id=1, source_target_pairs={{0,8},{4,12},{8,16},{12,20},{16,24},{20,28},{24,32},{28,36},{32,40... | collective-permute-start | bytes 1720328 | tf_op jit(solution)/shard_map/ppermute | solution.py:286
  687.0 60.9 %collective-permute-start.28 = (bf16[10,32,896]{2,1,0:T(8,128)(2,1)}, bf16[10,32,896]{2,1,0:T(8,128)(2,1)S(1)}, u32[]{:S(2)}, u32[]{:S(2)}) collective-permute-start(bf16[10,32,896]{2,1,0:T(8,128)(2,1)} %get-tuple-element.113), channel_id=1, source_target_pairs={{0,56},{4,60},{8,0},{12,4},{16,8},{20,12},{24,16},{28,20},{32,24},... | collective-permute-start | bytes 1720328 | tf_op jit(solution)/shard_map/ppermute | solution.py:287
  741.1 32.2 %collective-permute-start.14 = (bf16[10,32,896]{2,1,0:T(8,128)(2,1)}, bf16[10,32,896]{2,1,0:T(8,128)(2,1)S(1)}, u32[]{:S(2)}, u32[]{:S(2)}) collective-permute-start(bf16[10,32,896]{2,1,0:T(8,128)(2,1)} %get-tuple-element.98), channel_id=1, source_target_pairs={{0,8},{4,12},{8,16},{12,20},{16,24},{20,28},{24,32},{28,36},{32,40... | collective-permute-start | bytes 1720328 | tf_op jit(solution)/shard_map/ppermute | solution.py:286
  741.2 36.1 %collective-permute-start.15 = (bf16[10,32,896]{2,1,0:T(8,128)(2,1)}, bf16[10,32,896]{2,1,0:T(8,128)(2,1)S(1)}, u32[]{:S(2)}, u32[]{:S(2)}) collective-permute-start(bf16[10,32,896]{2,1,0:T(8,128)(2,1)} %get-tuple-element.99), channel_id=1, source_target_pairs={{0,56},{4,60},{8,0},{12,4},{16,8},{20,12},{24,16},{28,20},{32,24},... | collective-permute-start | bytes 1720328 | tf_op jit(solution)/shard_map/ppermute | solution.py:287
  746.6 3.8 copy-start.21
  746.6 140.3 %collective-permute-start = (s32[8,128]{1,0:T(8,128)S(1)}, s32[8,128]{1,0:T(8,128)S(1)}, u32[]{:S(2)}, u32[]{:S(2)}) collective-permute-start(s32[8,128]{1,0:T(8,128)S(1)} %broadcast_in_dim.93), channel_id=1, source_target_pairs={{0,1},{1,2},{2,3},{3,0},{4,5},{5,6},{6,7},{7,4},{8,9},{9,10},{10,1... | collective-permute-start | bytes 12296 | tf_op jit(solution)/shard_map/ppermute | solution.py:334
  747.8 142.4 %collective-permute-start.1 = (s32[8,128]{1,0:T(8,128)S(1)}, s32[8,128]{1,0:T(8,128)S(1)}, u32[]{:S(2)}, u32[]{:S(2)}) collective-permute-start(s32[8,128]{1,0:T(8,128)S(1)} %broadcast_in_dim.93), channel_id=1, source_target_pairs={{0,2},{1,3},{2,0},{3,1},{4,6},{5,7},{6,4},{7,5},{8,10},{9,11},{10,... | collective-permute-start | bytes 12296 | tf_op jit(solution)/shard_map/ppermute | solution.py:334
  773.3 4.0 copy-start.19
  773.3 118.2 %collective-permute-start.29 = (bf16[12,32,896]{2,1,0:T(8,128)(2,1)}, bf16[12,32,896]{2,1,0:T(8,128)(2,1)}, u32[]{:S(2)}, u32[]{:S(2)}) collective-permute-start(bf16[12,32,896]{2,1,0:T(8,128)(2,1)} %get-tuple-element.115), channel_id=1, source_target_pairs={{0,4},{4,0},{8,12},{12,8},{16,20},{20,16},{24,28},{28,24},{32,36},... | collective-permute-start | bytes 2064392 | tf_op jit(solution)/shard_map/ppermute | solution.py:291
  778.1 44.1 %copy-start.26 = (bf16[6,768]{1,0:T(8,128)(2,1)S(1)}, bf16[6,768]{1,0:T(8,128)(2,1)}, u32[]{:S(2)}) copy-start(bf16[6,768]{1,0:T(8,128)(2,1)} %param.27) | copy-start | bytes 27652
  822.0 66.8 %copy-start.18 = (bf16[384,2048]{1,0:T(8,128)(2,1)S(1)}, bf16[384,2048]{1,0:T(8,128)(2,1)}, u32[]{:S(2)}) copy-start(bf16[384,2048]{1,0:T(8,128)(2,1)} %param.31) | copy-start | bytes 4718596
  822.0 69.6 %collective-permute-start.16 = (bf16[12,32,896]{2,1,0:T(8,128)(2,1)}, bf16[12,32,896]{2,1,0:T(8,128)(2,1)}, u32[]{:S(2)}, u32[]{:S(2)}) collective-permute-start(bf16[12,32,896]{2,1,0:T(8,128)(2,1)} %get-tuple-element.101), channel_id=1, source_target_pairs={{0,4},{4,0},{8,12},{12,8},{16,20},{20,16},{24,28},{28,24},{32,36},... | collective-permute-start | bytes 2064392 | tf_op jit(solution)/shard_map/ppermute | solution.py:291
  886.9 3.4 collective-permute-start.2
  (20 other events, 22.5 us)
Sparse Core Ops, SparseCore 0:
  10.6 81.5 all-gather.3
